TPU v7x, 32 devices: a whole 2x2x4 slice. The times are simulated.
32 devices in a mesh: ctx: 4 (over y, x), head: 8 (over z, core).
Axes of the slice: x: 2, y: 2, z: 4, core: 2. Of those that a mesh axis runs over, the one named last changes fastest.
Arguments:
- passage_q: bfloat16 [4096, 16384], P(('ctx', 'head')), may hold values from -12 to 12
- passage_k: bfloat16 [4096, 1024], P(('ctx', 'head')), may hold values from -12 to 12
- passage_v: bfloat16 [4096, 1024], P(('ctx', 'head')), may hold values from -6 to 6
- new_q: bfloat16 [2048, 16384], P(('ctx', 'head')), may hold values from -12 to 12
- new_k: bfloat16 [2048, 1024], P(('ctx', 'head')), may hold values from -12 to 12
- new_v: bfloat16 [2048, 1024], P(('ctx', 'head')), may hold values from -6 to 6
- segments: int32 [4096], replicated, may hold values from 0 to 15, never falling along the last dimension, each value on 1 to 512 neighbouring positions
Outputs:
- passage_out: bfloat16 [4096, 16384], P(('ctx', 'head'))
- new_out: bfloat16 [2048, 16384], P(('ctx', 'head'))
Inputs may be any that keep to these rules, and one draw needn't show every extreme that they name: `segments`: passages are runs of equal numbers, rising by one from run to run, each of 1 to 512 tokens; some passage has exactly 512.
All inputs are finite; a program needn't handle non-finite values.
Results may differ from a plain program's by a relative error of at most 0.008.
Values may be sent and summed in bfloat16 or wider, within the bound.
A program may use at most 192 MiB of HBM per device.

v0:
```python
import jax
import jax.numpy as jnp
from jax import lax
from jax.sharding import PartitionSpec as P

QH = 128
KVH = 8
HD = 128
MOST = 512


big_neg = -1e30


def shifted(block, axis, distance):
    devices = range(lax.axis_size(axis))
    route = [(i - distance, i) for i in devices if i - distance in devices]
    return lax.ppermute(block, axis, route)


def attend(q_block, k_block, v_block, visible):
    scores = jnp.einsum(
        "qhd,kd->qhk", q_block, k_block, preferred_element_type=jnp.float32
    ) * HD ** (-0.5)
    if visible is None:
        row_max = jnp.max(scores, axis=-1)
        weights = jnp.exp(scores - row_max[..., None])
    else:
        masked = jnp.where(visible[:, None, :], scores, big_neg)
        row_max = jnp.max(masked, axis=-1)
        weights = jnp.where(visible[:, None, :], jnp.exp(masked - row_max[..., None]), 0.0)
    row_sum = jnp.sum(weights, axis=-1)
    weighted = jnp.einsum(
        "qhk,kd->qhd", weights.astype(jnp.bfloat16), v_block, preferred_element_type=jnp.float32
    )
    return (weighted, row_max, row_sum)


def combine_parts(first_part, second_part):
    top_max = jnp.maximum(first_part[1], second_part[1])
    first_w = jnp.exp(first_part[1] - top_max)
    second_w = jnp.exp(second_part[1] - top_max)
    weighted = first_part[0] * first_w[..., None] + second_part[0] * second_w[..., None]
    return (weighted, top_max, first_part[2] * first_w + second_part[2] * second_w)


def local_passages(passage_q, passage_k, passage_v, segments, head_count):
    flat_index = lax.axis_index("ctx") * head_count + lax.axis_index("head")
    row_count = passage_k.shape[0]
    group_size = QH // KVH
    hops = max(1, (MOST - 1 + row_count - 1) // row_count)
    window = hops * row_count
    empty = jnp.zeros((window, KVH * HD), jnp.bfloat16)

    def hop(step, carry):
        moving_k, moving_v, buffer_k, buffer_v = carry
        moving_k, moving_v = shifted((moving_k, moving_v), ("ctx", "head"), 1)
        place = ((hops - 1 - step) * row_count).astype(jnp.int32)
        buffer_k = lax.dynamic_update_slice_in_dim(buffer_k, moving_k, place, 0)
        buffer_v = lax.dynamic_update_slice_in_dim(buffer_v, moving_v, place, 0)
        return (moving_k, moving_v, buffer_k, buffer_v)

    carried = lax.fori_loop(0, hops, hop, (passage_k, passage_v, empty, empty))
    keys_ext = jnp.concatenate([carried[2], passage_k], axis=0).reshape(window + row_count, KVH, HD)
    vals_ext = jnp.concatenate([carried[3], passage_v], axis=0).reshape(window + row_count, KVH, HD)
    seg_padded = jnp.concatenate([jnp.full((window,), -1, jnp.int32), segments])
    seg_key = lax.dynamic_slice_in_dim(seg_padded, flat_index * row_count, window + row_count, 0)
    seg_query = seg_key[window:]
    causal = jnp.arange(window + row_count)[None, :] - window <= jnp.arange(row_count)[:, None]
    visible = causal & (seg_query[:, None] == seg_key[None, :])
    q_heads = jnp.transpose(passage_q.reshape(row_count, KVH, group_size, HD), (1, 0, 2, 3))
    k_heads = jnp.transpose(keys_ext, (1, 0, 2))
    v_heads = jnp.transpose(vals_ext, (1, 0, 2))

    def per_head(inputs):
        q_head, k_head, v_head = inputs
        weighted, row_max, row_sum = attend(q_head, k_head, v_head, visible)
        return (weighted / row_sum[..., None]).astype(jnp.bfloat16)

    outputs = lax.map(per_head, (q_heads, k_heads, v_heads))
    return jnp.transpose(outputs, (1, 0, 2, 3)).reshape(row_count, QH * HD)


def on_device(passage_q, passage_k, passage_v, new_q, new_k, new_v, segments):
    head_count = lax.axis_size("head")
    ctx_count = lax.axis_size("ctx")
    ctx_index = lax.axis_index("ctx")
    heads_local = QH // head_count
    copy_count = head_count // KVH

    def spread(kv_rows):
        row_count = kv_rows.shape[0]
        return jnp.repeat(kv_rows.reshape(row_count, KVH, HD), copy_count, axis=1).reshape(
            row_count, head_count * HD
        )

    fresh_q, fresh_k, fresh_v, pass_k, pass_v = (
        lax.all_to_all(new_q, "head", split_axis=1, concat_axis=0, tiled=True),
        lax.all_to_all(spread(new_k), "head", split_axis=1, concat_axis=0, tiled=True),
        lax.all_to_all(spread(new_v), "head", split_axis=1, concat_axis=0, tiled=True),
        lax.all_to_all(spread(passage_k), "head", split_axis=1, concat_axis=0, tiled=True),
        lax.all_to_all(spread(passage_v), "head", split_axis=1, concat_axis=0, tiled=True),
    )
    pass_out = local_passages(passage_q, passage_k, passage_v, segments, head_count)
    new_local = fresh_q.shape[0]
    all_queries = lax.all_gather(fresh_q, "ctx", axis=0, tiled=True)
    total_new = all_queries.shape[0]
    query_rows = min(512, total_new)
    query_groups = all_queries.reshape(total_new // query_rows, query_rows, heads_local, HD)
    key_pos = ctx_index * new_local + jnp.arange(new_local, dtype=jnp.int32)

    def partial_block(inputs):
        q_block, block_id = inputs
        passage_part = attend(q_block, pass_k, pass_v, None)
        query_pos = block_id * query_rows + jnp.arange(query_rows, dtype=jnp.int32)
        visible = key_pos[None, :] <= query_pos[:, None]
        return combine_parts(passage_part, attend(q_block, fresh_k, fresh_v, visible))

    weighted, row_max, row_sum = lax.map(
        partial_block, (query_groups, jnp.arange(total_new // query_rows, dtype=jnp.int32))
    )
    weighted = weighted.reshape(1, total_new, heads_local * HD)
    row_max = row_max.reshape(1, total_new, heads_local)
    row_sum = row_sum.reshape(1, total_new, heads_local)
    parts_w, parts_max, parts_sum = (
        lax.all_to_all(weighted, "ctx", split_axis=1, concat_axis=0, tiled=True),
        lax.all_to_all(row_max, "ctx", split_axis=1, concat_axis=0, tiled=True),
        lax.all_to_all(row_sum, "ctx", split_axis=1, concat_axis=0, tiled=True),
    )
    top_max = jnp.max(parts_max, axis=0)
    factors = jnp.exp(parts_max - top_max[None])
    numer_sum = jnp.sum(
        parts_w.reshape(ctx_count, new_local, heads_local, HD) * factors[..., None], axis=0
    )
    denom_sum = jnp.sum(parts_sum * factors, axis=0)
    fresh_out = (
        (numer_sum / denom_sum[..., None]).astype(jnp.bfloat16).reshape(new_local, heads_local * HD)
    )
    fresh_rows_out = lax.all_to_all(fresh_out, "head", split_axis=0, concat_axis=1, tiled=True)
    return (pass_out, fresh_rows_out)


def solution(mesh):
    in_specs = (
        P(("ctx", "head"), None),
        P(("ctx", "head"), None),
        P(("ctx", "head"), None),
        P(("ctx", "head"), None),
        P(("ctx", "head"), None),
        P(("ctx", "head"), None),
        P(),
    )
    out_specs = (P(("ctx", "head"), None), P(("ctx", "head"), None))
    return jax.shard_map(
        on_device, mesh=mesh, in_specs=in_specs, out_specs=out_specs, check_vma=False
    )
```

profile of v0, /device:TPU:0, one launch (start us, length us, event | category | flops | bytes accessed | tf_op | source)
XLA Modules:
  0.0 816.2 jit_solution(15665739036683545103)
XLA Ops:
  11.1 55.4 %all_to_all.147 = bf16[64,8,2048]{2,0,1:T(8,128)(2,1)} all-to-all(bf16[64,8,2048]{2,0,1:T(8,128)(2,1)S(1)} %bitcast.214), channel_id=1, replica_groups=mesh['ctx'=4,'head'=8] {'head'}, dimensions={1} | all-to-all | bytes 4194304 | tf_op jit(solution)/shard_map/all_to_all | solution.py:98
  71.3 6.0 all-to-all-done.3
  91.6 8.9 %all-to-all-done.1 = bf16[128,8,128]{2,0,1:T(8,128)(2,1)S(1)} async-done(((bf16[128,8,128]{2,0,1:T(8,128)(2,1)}), bf16[128,8,128]{2,0,1:T(8,128)(2,1)S(1)}, u32[]{:S(2)}, u32[]{:S(2)}) %all-to-all-start.1) | async-done | bytes 262176 | tf_op jit(solution)/shard_map/all_to_all | solution.py:101
  103.9 49.3 %all-gather.2.cloned.1.call-done = bf16[2048,2048]{1,0:T(8,128)(2,1)} async-done(((bf16[512,2048]{1,0:T(8,128)(2,1)}), bf16[2048,2048]{1,0:T(8,128)(2,1)}) %all-gather.2.cloned.1.call-update) | async-done | bytes 8388624 | tf_op jit(solution)/shard_map/all_gather | solution.py:106
  153.2 9.7 %copy.199 = bf16[256,8,16,128]{3,2,1,0:T(8,128)(2,1)} copy(bf16[256,8,16,128]{3,1,2,0:T(8,128)(2,1)} %bitcast.211) | data formatting | bytes 16777216
  163.0 275.6 %while.47 = (s32[]{:T(128)}, f32[4,512,16,128]{3,2,1,0:T(8,128)}, f32[4,512,16]{1,2,0:T(8,128)S(1)}, f32[4,512,16]{1,2,0:T(8,128)S(1)}, bf16[4,512,16,128]{3,2,1...) while((s32[]{:T(128)}, f32[4,512,16,128]{3,2,1,0:T(8,128)}, ...), condition=%wide.region_11.12_spmd.clone, body=%wide.region_6.11_spmd.clone.sunk | while | flops 6567535616 | bytes 251011856 | solution.py:119
  176.5 13.2 %multiply_reduce_fusion.4 = (f32[512,16]{0,1:T(8,128)S(1)}, f32[512,16,1024]{2,0,1:T(8,128)}) fusion(bf16[1024,128]{1,0:T(8,128)(2,1)S(1)} %get-tuple-element.679, bf16[1,512,16,128]{3,2,1,0:T(8,128)(2,1)S(1)} %constant_dynamic-slice_fusion.2), kind=kOutput, calls=%fused_computation.37.clone.1 | convolution fusion | flops 2164252672 | bytes 35946496 | tf_op jit(solution)/shard_map/while/body/eval_jaxpr/qhd,kd->qhk/dot_general | solution.py:22
  189.6 14.2 %fusion.131 = f32[512,16]{0,1:T(8,128)S(1)} fusion(f32[512,16,1024]{2,0,1:T(8,128)} %get-tuple-element.581, f32[512,16]{0,1:T(8,128)S(1)} %get-tuple-element.582), kind=kLoop, calls=%fused_computation.38.clone.1 | loop fusion | flops 25157632 | bytes 33619968 | tf_op jit(solution)/shard_map/while/body/eval_jaxpr/reduce_sum | solution.py:32
  204.0 12.7 %fusion.127 = f32[512,16,128]{2,0,1:T(8,128)S(1)} fusion(f32[512,16,1024]{2,0,1:T(8,128)} %get-tuple-element.581, f32[512,16]{0,1:T(8,128)S(1)} %get-tuple-element.582, bf16[1024,128]{1,0:T(8,128)(2,1)S(1)} %get-tuple-element.680), kind=kOutput, calls=%fused_computation.40.clone.1 | convolution fusion | flops 2172649472 | bytes 38043648 | tf_op jit(solution)/shard_map/while/body/eval_jaxpr/qhk,kd->qhd/dot_general | solution.py:33
  216.6 11.2 %add_bitcast_fusion.2 = f32[1,512,16,128]{3,1,2,0:T(8,128)S(1)} fusion(f32[512,16,128]{2,0,1:T(8,128)S(1)} %fusion.127, f32[512,16]{0,1:T(8,128)S(1)} %get-tuple-element.586, f32[512,16]{0,1:T(8,128)S(1)} %get-tuple-element.587, f32[512,16,512]{0,2,1:T(8,128)} %copy-done.2, f32[512,16]{0,1:T(8,128)S(1)} %get-tuple-element.585, ...), kind=kOutput, calls=%fused_computation.51.clone.1 | convolution fusion | flops 1097859072 | bytes 25657344 | tf_op jit(solution)/shard_map/while/body/eval_jaxpr/qhk,kd->qhd/dot_general | solution.py:33
  245.3 13.2 %multiply_reduce_fusion.4 = (f32[512,16]{0,1:T(8,128)S(1)}, f32[512,16,1024]{2,0,1:T(8,128)}) fusion(bf16[1024,128]{1,0:T(8,128)(2,1)S(1)} %get-tuple-element.679, bf16[1,512,16,128]{3,2,1,0:T(8,128)(2,1)S(1)} %constant_dynamic-slice_fusion.2), kind=kOutput, calls=%fused_computation.37.clone.1 | convolution fusion | flops 2164252672 | bytes 35946496 | tf_op jit(solution)/shard_map/while/body/eval_jaxpr/qhd,kd->qhk/dot_general | solution.py:22
  258.5 14.2 %fusion.131 = f32[512,16]{0,1:T(8,128)S(1)} fusion(f32[512,16,1024]{2,0,1:T(8,128)} %get-tuple-element.581, f32[512,16]{0,1:T(8,128)S(1)} %get-tuple-element.582), kind=kLoop, calls=%fused_computation.38.clone.1 | loop fusion | flops 25157632 | bytes 33619968 | tf_op jit(solution)/shard_map/while/body/eval_jaxpr/reduce_sum | solution.py:32
  272.8 12.7 %fusion.127 = f32[512,16,128]{2,0,1:T(8,128)S(1)} fusion(f32[512,16,1024]{2,0,1:T(8,128)} %get-tuple-element.581, f32[512,16]{0,1:T(8,128)S(1)} %get-tuple-element.582, bf16[1024,128]{1,0:T(8,128)(2,1)S(1)} %get-tuple-element.680), kind=kOutput, calls=%fused_computation.40.clone.1 | convolution fusion | flops 2172649472 | bytes 38043648 | tf_op jit(solution)/shard_map/while/body/eval_jaxpr/qhk,kd->qhd/dot_general | solution.py:33
  285.4 11.2 %add_bitcast_fusion.2 = f32[1,512,16,128]{3,1,2,0:T(8,128)S(1)} fusion(f32[512,16,128]{2,0,1:T(8,128)S(1)} %fusion.127, f32[512,16]{0,1:T(8,128)S(1)} %get-tuple-element.586, f32[512,16]{0,1:T(8,128)S(1)} %get-tuple-element.587, f32[512,16,512]{0,2,1:T(8,128)} %copy-done.2, f32[512,16]{0,1:T(8,128)S(1)} %get-tuple-element.585, ...), kind=kOutput, calls=%fused_computation.51.clone.1 | convolution fusion | flops 1097859072 | bytes 25657344 | tf_op jit(solution)/shard_map/while/body/eval_jaxpr/qhk,kd->qhd/dot_general | solution.py:33
  314.0 13.2 %multiply_reduce_fusion.4 = (f32[512,16]{0,1:T(8,128)S(1)}, f32[512,16,1024]{2,0,1:T(8,128)}) fusion(bf16[1024,128]{1,0:T(8,128)(2,1)S(1)} %get-tuple-element.679, bf16[1,512,16,128]{3,2,1,0:T(8,128)(2,1)S(1)} %constant_dynamic-slice_fusion.2), kind=kOutput, calls=%fused_computation.37.clone.1 | convolution fusion | flops 2164252672 | bytes 35946496 | tf_op jit(solution)/shard_map/while/body/eval_jaxpr/qhd,kd->qhk/dot_general | solution.py:22
  327.2 14.2 %fusion.131 = f32[512,16]{0,1:T(8,128)S(1)} fusion(f32[512,16,1024]{2,0,1:T(8,128)} %get-tuple-element.581, f32[512,16]{0,1:T(8,128)S(1)} %get-tuple-element.582), kind=kLoop, calls=%fused_computation.38.clone.1 | loop fusion | flops 25157632 | bytes 33619968 | tf_op jit(solution)/shard_map/while/body/eval_jaxpr/reduce_sum | solution.py:32
  341.5 12.7 %fusion.127 = f32[512,16,128]{2,0,1:T(8,128)S(1)} fusion(f32[512,16,1024]{2,0,1:T(8,128)} %get-tuple-element.581, f32[512,16]{0,1:T(8,128)S(1)} %get-tuple-element.582, bf16[1024,128]{1,0:T(8,128)(2,1)S(1)} %get-tuple-element.680), kind=kOutput, calls=%fused_computation.40.clone.1 | convolution fusion | flops 2172649472 | bytes 38043648 | tf_op jit(solution)/shard_map/while/body/eval_jaxpr/qhk,kd->qhd/dot_general | solution.py:33
  354.2 11.2 %add_bitcast_fusion.2 = f32[1,512,16,128]{3,1,2,0:T(8,128)S(1)} fusion(f32[512,16,128]{2,0,1:T(8,128)S(1)} %fusion.127, f32[512,16]{0,1:T(8,128)S(1)} %get-tuple-element.586, f32[512,16]{0,1:T(8,128)S(1)} %get-tuple-element.587, f32[512,16,512]{0,2,1:T(8,128)} %copy-done.2, f32[512,16]{0,1:T(8,128)S(1)} %get-tuple-element.585, ...), kind=kOutput, calls=%fused_computation.51.clone.1 | convolution fusion | flops 1097859072 | bytes 25657344 | tf_op jit(solution)/shard_map/while/body/eval_jaxpr/qhk,kd->qhd/dot_general | solution.py:33
  382.7 13.2 %multiply_reduce_fusion.4 = (f32[512,16]{0,1:T(8,128)S(1)}, f32[512,16,1024]{2,0,1:T(8,128)}) fusion(bf16[1024,128]{1,0:T(8,128)(2,1)S(1)} %get-tuple-element.679, bf16[1,512,16,128]{3,2,1,0:T(8,128)(2,1)S(1)} %constant_dynamic-slice_fusion.2), kind=kOutput, calls=%fused_computation.37.clone.1 | convolution fusion | flops 2164252672 | bytes 35946496 | tf_op jit(solution)/shard_map/while/body/eval_jaxpr/qhd,kd->qhk/dot_general | solution.py:22
  395.8 14.2 %fusion.131 = f32[512,16]{0,1:T(8,128)S(1)} fusion(f32[512,16,1024]{2,0,1:T(8,128)} %get-tuple-element.581, f32[512,16]{0,1:T(8,128)S(1)} %get-tuple-element.582), kind=kLoop, calls=%fused_computation.38.clone.1 | loop fusion | flops 25157632 | bytes 33619968 | tf_op jit(solution)/shard_map/while/body/eval_jaxpr/reduce_sum | solution.py:32
  410.2 12.7 %fusion.127 = f32[512,16,128]{2,0,1:T(8,128)S(1)} fusion(f32[512,16,1024]{2,0,1:T(8,128)} %get-tuple-element.581, f32[512,16]{0,1:T(8,128)S(1)} %get-tuple-element.582, bf16[1024,128]{1,0:T(8,128)(2,1)S(1)} %get-tuple-element.680), kind=kOutput, calls=%fused_computation.40.clone.1 | convolution fusion | flops 2172649472 | bytes 38043648 | tf_op jit(solution)/shard_map/while/body/eval_jaxpr/qhk,kd->qhd/dot_general | solution.py:33
  422.8 11.2 %add_bitcast_fusion.2 = f32[1,512,16,128]{3,1,2,0:T(8,128)S(1)} fusion(f32[512,16,128]{2,0,1:T(8,128)S(1)} %fusion.127, f32[512,16]{0,1:T(8,128)S(1)} %get-tuple-element.586, f32[512,16]{0,1:T(8,128)S(1)} %get-tuple-element.587, f32[512,16,512]{0,2,1:T(8,128)} %copy-done.2, f32[512,16]{0,1:T(8,128)S(1)} %get-tuple-element.585, ...), kind=kOutput, calls=%fused_computation.51.clone.1 | convolution fusion | flops 1097859072 | bytes 25657344 | tf_op jit(solution)/shard_map/while/body/eval_jaxpr/qhk,kd->qhd/dot_general | solution.py:33
  439.4 9.3 %reduce.3 = f32[2048,16]{1,0:T(8,128)S(1)} reduce(f32[2048,1,16]{2,1,0:T(1,128)S(1)} %bitcast.216, f32[]{:T(128)} %broadcast.88), dimensions={1}, to_apply=%bitcast.137.reduce_sub_computation | reduce | bytes 262148
  453.4 9.3 %reduce.1 = f32[2048,16]{1,0:T(8,128)S(1)} reduce(f32[2048,1,16]{2,1,0:T(1,128)S(1)} %bitcast.217, f32[]{:T(128)} %broadcast.88), dimensions={1}, to_apply=%bitcast.139.reduce_sub_computation | reduce | bytes 262148
  463.0 9.1 %all_to_all.148 = f32[4,1,8192]{2,1,0:T(1,128)} all-to-all(f32[4,1,8192]{2,1,0:T(1,128)S(1)} %reshape.213), channel_id=1, replica_groups=mesh['ctx'=4,'head'=8] {'ctx'}, dimensions={0} | all-to-all | bytes 262144 | tf_op jit(solution)/shard_map/all_to_all | solution.py:128
  472.1 7.3 all-to-all-start.5
  481.3 6.4 copy.139
  487.8 39.4 %while.45 = (s32[]{:T(128)}, bf16[128,1024]{1,0:T(8,128)(2,1)S(1)}, bf16[128,1024]{1,0:T(8,128)(2,1)S(1)}, bf16[512,1024]{0,1:T(8,128)(2,1)S(1)}, bf16[512,1024]...) while((s32[]{:T(128)}, bf16[128,1024]{1,0:T(8,128)(2,1)S(1)}, ...), condition=%wide.region_1.0_spmd, body=%wide.region_0.0_spmd.sunk | while | flops 7 | bytes 5243127 | solution.py:63
  545.8 136.9 %all-to-all-done.5 = f32[1,2048,2048]{2,0,1:T(1,128)} async-done(((f32[1,2048,2048]{2,0,1:T(1,128)}), f32[1,2048,2048]{2,0,1:T(1,128)}, u32[]{:S(2)}, u32[]{:S(2)}) %all-to-all-start.5) | async-done | bytes 16777248 | tf_op jit(solution)/shard_map/all_to_all | solution.py:126
  682.7 6.3 mul.96
  689.0 31.7 %multiply_reduce_fusion.1 = f32[512,2048]{1,0:T(8,128)S(1)} fusion(f32[1,4,512,2048]{3,0,2,1:T(1,128)} %bitcast.18, f32[1,4,512,2048]{3,0,2,1:T(1,128)} %bitcast.202), kind=kLoop, calls=%fused_computation.81 | loop fusion | flops 7340032 | bytes 37748736 | tf_op jit(solution)/shard_map/reduce_sum | solution.py:132
  729.1 67.9 %while.46 = (s32[]{:T(128)}, bf16[8,128,16,128]{3,1,2,0:T(8,128)(2,1)}, bf16[8,128,16,128]{1,3,2,0:T(8,128)(2,1)}, bf16[8,640,128]{1,2,0:T(8,128)(2,1)}, bf16[8,...) while((s32[]{:T(128)}, ...), condition=%wide.region_5.6_spmd.clone, body=%wide.region_2.5_spmd.clone.sunk | while | flops 679723648 | bytes 6889053 | solution.py:80
  (200 shorter events, 246.8 us)
Async XLA Ops:
  7.2 59.4 %copy-start = (bf16[64,1024]{1,0:T(8,128)(2,1)S(1)}, bf16[64,1024]{1,0:T(8,128)(2,1)}, u32[]{:S(2)}) copy-start(bf16[64,1024]{1,0:T(8,128)(2,1)} %param.17) | copy-start | bytes 393220
  7.2 146.0 %all-gather.2.cloned.1.call-start = ((), (), s32[]{:S(2)}) async-start(), calls=%async_computation.9 | async-start | bytes 10485760 | tf_op jit(solution)/shard_map/all_gather | solution.py:106
  8.2 72.5 %copy-start.3 = (bf16[128,1024]{1,0:T(8,128)(2,1)}, bf16[128,1024]{1,0:T(8,128)(2,1)S(1)}, u32[]{:S(2)}) copy-start(bf16[128,1024]{1,0:T(8,128)(2,1)S(1)} %copy.265) | copy-start | bytes 786436
  9.3 81.6 %copy-start.5 = (bf16[128,1024]{1,0:T(8,128)(2,1)}, bf16[128,1024]{1,0:T(8,128)(2,1)S(1)}, u32[]{:S(2)}) copy-start(bf16[128,1024]{1,0:T(8,128)(2,1)S(1)} %copy.266) | copy-start | bytes 786436
  11.1 59.5 %copy-start.10 = (bf16[64,1024]{1,0:T(8,128)(2,1)S(1)}, bf16[64,1024]{1,0:T(8,128)(2,1)}, u32[]{:S(2)}) copy-start(bf16[64,1024]{1,0:T(8,128)(2,1)} %param.18) | copy-start | bytes 393220
  67.2 10.1 %all-to-all-start.3 = ((bf16[64,8,128]{2,0,1:T(8,128)(2,1)}), bf16[64,8,128]{2,0,1:T(8,128)(2,1)S(1)}, u32[]{:S(2)}, u32[]{:S(2)}) async-start(bf16[64,8,128]{2,0,1:T(8,128)(2,1)} %copy_bitcast_fusion.8), calls=%async_computation.3 | async-start | bytes 262144 | tf_op jit(solution)/shard_map/all_to_all | solution.py:99
  77.3 10.1 %all-to-all-start.4 = ((bf16[64,8,128]{2,0,1:T(8,128)(2,1)}), bf16[64,8,128]{2,0,1:T(8,128)(2,1)S(1)}, u32[]{:S(2)}, u32[]{:S(2)}) async-start(bf16[64,8,128]{2,0,1:T(8,128)(2,1)} %copy_bitcast_fusion.7), calls=%async_computation.4 | async-start | bytes 262144 | tf_op jit(solution)/shard_map/all_to_all | solution.py:100
  87.4 13.1 %all-to-all-start.1 = ((bf16[128,8,128]{2,0,1:T(8,128)(2,1)}), bf16[128,8,128]{2,0,1:T(8,128)(2,1)S(1)}, u32[]{:S(2)}, u32[]{:S(2)}) async-start(bf16[128,8,128]{2,0,1:T(8,128)(2,1)} %copy_bitcast_fusion.6), calls=%async_computation.1 | async-start | bytes 524288 | tf_op jit(solution)/shard_map/all_to_all | solution.py:101
  100.5 62.5 %all-to-all-start.2 = ((bf16[128,8,128]{2,0,1:T(8,128)(2,1)}), bf16[128,8,128]{2,0,1:T(8,128)(2,1)S(1)}, u32[]{:S(2)}, u32[]{:S(2)}) async-start(bf16[128,8,128]{2,0,1:T(8,128)(2,1)} %copy_bitcast_fusion.5), calls=%async_computation.2 | async-start | bytes 524288 | tf_op jit(solution)/shard_map/all_to_all | solution.py:102
  170.8 5.7 copy-start.2
  227.8 4.5 copy-start.12
  239.6 5.7 copy-start.2
  296.6 4.4 copy-start.12
  308.3 5.7 copy-start.2
  377.0 5.7 copy-start.2
  449.7 13.3 %all-to-all-start.6 = ((f32[4,1,8192]{2,1,0:T(1,128)}), f32[4,1,8192]{2,1,0:T(1,128)S(1)}, u32[]{:S(2)}, u32[]{:S(2)}) async-start(f32[4,1,8192]{2,1,0:T(1,128)} %reshape.211), calls=%async_computation.6 | async-start | bytes 262144 | tf_op jit(solution)/shard_map/all_to_all | solution.py:127
  463.0 9.1 %copy-start.7 = (f32[4,1,8192]{2,1,0:T(1,128)}, f32[4,1,8192]{2,1,0:T(1,128)S(1)}, u32[]{:S(2)}) copy-start(f32[4,1,8192]{2,1,0:T(1,128)S(1)} %all-to-all-done.6) | copy-start | bytes 393220
  472.1 7.3 copy-start.4
  472.1 8.2 %copy-start.6 = (bf16[128,1024]{1,0:T(8,128)(2,1)S(1)}, bf16[128,1024]{1,0:T(8,128)(2,1)}, u32[]{:S(2)}) copy-start(bf16[128,1024]{1,0:T(8,128)(2,1)} %copy-done.5) | copy-start | bytes 786436
  472.1 9.0 %copy-start.13 = (s32[4096]{0:T(1024)S(1)}, s32[4096]{0:T(1024)}, u32[]{:S(2)}) copy-start(s32[4096]{0:T(1024)} %param.19) | copy-start | bytes 49156
  472.1 210.6 %all-to-all-start.5 = ((f32[1,2048,2048]{2,0,1:T(1,128)}), f32[1,2048,2048]{2,0,1:T(1,128)}, u32[]{:S(2)}, u32[]{:S(2)}) async-start(f32[1,2048,2048]{2,0,1:T(1,128)} %bitcast.205), calls=%async_computation.5 | async-start | bytes 33554432 | tf_op jit(solution)/shard_map/all_to_all | solution.py:126
  487.8 5.5 collective-permute-start
  489.2 5.3 collective-permute-start.1
  494.7 9.4 %collective-permute-start = (bf16[128,1024]{1,0:T(8,128)(2,1)S(1)}, bf16[128,1024]{1,0:T(8,128)(2,1)S(1)}, u32[]{:S(2)}, u32[]{:S(2)}) collective-permute-start(bf16[128,1024]{1,0:T(8,128)(2,1)S(1)} %get-tuple-element.602), channel_id=1, source_target_pairs={{0,1},{1,2},{2,3},{3,4},{4,5},{5,6},{6,7},{7,8},{8,9},{9,10},{10,1... | collective-permute-start | bytes 786440 | tf_op jit(solution)/shard_map/while/body/eval_jaxpr/ppermute | solution.py:18
  499.7 5.5 collective-permute-start.1
  505.6 9.4 %collective-permute-start = (bf16[128,1024]{1,0:T(8,128)(2,1)S(1)}, bf16[128,1024]{1,0:T(8,128)(2,1)S(1)}, u32[]{:S(2)}, u32[]{:S(2)}) collective-permute-start(bf16[128,1024]{1,0:T(8,128)(2,1)S(1)} %get-tuple-element.602), channel_id=1, source_target_pairs={{0,1},{1,2},{2,3},{3,4},{4,5},{5,6},{6,7},{7,8},{8,9},{9,10},{10,1... | collective-permute-start | bytes 786440 | tf_op jit(solution)/shard_map/while/body/eval_jaxpr/ppermute | solution.py:18
  510.5 5.5 collective-permute-start.1
  516.4 9.4 %collective-permute-start = (bf16[128,1024]{1,0:T(8,128)(2,1)S(1)}, bf16[128,1024]{1,0:T(8,128)(2,1)S(1)}, u32[]{:S(2)}, u32[]{:S(2)}) collective-permute-start(bf16[128,1024]{1,0:T(8,128)(2,1)S(1)} %get-tuple-element.602), channel_id=1, source_target_pairs={{0,1},{1,2},{2,3},{3,4},{4,5},{5,6},{6,7},{7,8},{8,9},{9,10},{10,1... | collective-permute-start | bytes 786440 | tf_op jit(solution)/shard_map/while/body/eval_jaxpr/ppermute | solution.py:18
  521.4 5.5 collective-permute-start.1
  527.2 7.6 copy-start.9
  725.3 82.3 %all-to-all-start.8 = ((bf16[8,64,2048]{2,1,0:T(8,128)(2,1)}), bf16[8,64,2048]{2,1,0:T(8,128)(2,1)S(1)}, u32[]{:S(2)}, u32[]{:S(2)}) async-start(bf16[8,64,2048]{2,1,0:T(8,128)(2,1)} %divide_convert_fusion), calls=%async_computation.8 | async-start | bytes 4194304 | tf_op jit(solution)/shard_map/all_to_all | solution.py:139
  802.0 7.1 copy-start.1
  (7 other events, 18.0 us)
Sparse Core Ops, SparseCore 0:
  66.7 86.5 all-gather.1
where the time goes:
time: 822 us; the launch traced here: 816 us
  matrix products  230 us (28%)
  waiting for transfers between devices  211 us (26%)
  other arithmetic  136 us (17%)
  local copies, waits for them, and re-layouts  94.5 us (11%)
  blocking collectives  64.5 us (8%)
  starting transfers between devices  61.6 us (7%)
  between operations  14.6 us (2%)
    all_to_all x1, waiting for transfers between devices, on_device(): lax.all_to_all(weighted, 'ctx', split_axis=1, concat_axis=0, tiled=True)  137 us
    dot_general x16, matrix products, attend(): jnp.einsum('qhk,kd->qhd', weights.astype(jnp.bfloat16), v_block, preferre...  122 us
    reduce_sum x8, other arithmetic, attend(): row_sum = jnp.sum(weights, axis=-1)  73 us
    dot_general x8, matrix products, attend(): jnp.einsum('qhd,kd->qhk', q_block, k_block, preferred_element_type=jnp.fl...  68 us
    all_to_all x1, blocking collectives, on_device(): lax.all_to_all(new_q, 'head', split_axis=1, concat_axis=0, tiled=True)  55.4 us
    all_gather x1, waiting for transfers between devices, on_device(): all_queries = lax.all_gather(fresh_q, 'ctx', axis=0, tiled=True)  49.3 us
    sub x8, matrix products, attend(): masked - row_max[..., None]  39.7 us
    ppermute x8, starting transfers between devices, shifted(): return lax.ppermute(block, axis, route)  33.5 us
  transfers between devices with their start and end apart: 16, of which 9 were waited for; matrix products, arithmetic and copies ran while one was open for 16% of the time, Pallas kernels for 0%

commit v1 on v0

v1 whole, which is shorter than its diff:
```python
import functools
import math

import jax
import jax.numpy as jnp
from jax import lax
from jax.experimental import pallas as pl
from jax.experimental.pallas import tpu as pltpu
from jax.sharding import Mesh, PartitionSpec as P

QH = 128
KVH = 8
HD = 128
MOST = 512
CORES = 2
NEG = -1e30
SCALE = HD ** -0.5 * math.log2(math.e)
DIMS_T = (((1,), (1,)), ((), ()))


def scores_of(q, k):
    return lax.dot_general(q, k, DIMS_T, preferred_element_type=jnp.float32)


def question_kernel(groups, key_block, z_ref, q_ref, pk_ref, pv_ref, nk_ref, nv_ref, o_ref, pva, nva, acc, top):
    rows = q_ref.shape[0]
    run = rows // groups
    passage = pk_ref.shape[0]
    span = nk_ref.shape[0] // groups

    @pl.when(pl.program_id(0) == 0)
    def _():
        pva[:, :HD] = pv_ref[...]
        pva[:, HD:] = jnp.ones((passage, HD), jnp.bfloat16)
        nva[:, :HD] = nv_ref[...]
        nva[:, HD:] = jnp.ones((span * groups, HD), jnp.bfloat16)

    jobs = [(pk_ref, pva, i * key_block, key_block, 0, False) for i in range(passage // key_block)]
    jobs += [(nk_ref, nva, b * span, span, b * run, True) for b in range(groups)]

    def scored(job):
        k_ref, _, at, size, first, own = job
        s = scores_of(q_ref[first:, :], k_ref[at:at + size, :])
        if own:
            here = lax.broadcasted_iota(jnp.int32, (run, size), 0) + z_ref[0] * run
            there = lax.broadcasted_iota(jnp.int32, (run, size), 1)
            edge = jnp.where(there <= here, s[:run], NEG)
            s = edge if first + run == rows else jnp.concatenate([edge, s[run:]], axis=0)
        return s

    s = scored(jobs[0])
    for i, job in enumerate(jobs):
        later = scored(jobs[i + 1]) if i + 1 < len(jobs) else None
        _, v_ref, at, size, first, own = job
        best = jnp.max(s, axis=1, keepdims=True)
        if i > 0:
            before = top[first:, :]
            best = jnp.maximum(before[:, :1], best)
        wide = jnp.broadcast_to(best, (rows - first, HD))
        p = jnp.exp2(s * SCALE - best * SCALE).astype(jnp.bfloat16)
        part = jnp.dot(p, v_ref[at:at + size, :], preferred_element_type=jnp.float32)
        if i > 0:
            shrink = jnp.exp2((before - wide) * SCALE)
            acc[first:, :HD] = acc[first:, :HD] * shrink + part[:, :HD]
            acc[first:, HD:] = acc[first:, HD:] * shrink + part[:, HD:]
        else:
            acc[...] = part
        top[first:, :] = wide
        s = later
    o_ref[...] = (acc[:, :HD] / acc[:, HD:]).astype(jnp.bfloat16)


def question_attention(z_index, q, pk, pv, nk, nv, groups):
    rows, columns = q.shape
    heads = columns // HD
    passage, new = pk.shape[0], nk.shape[0]
    key_block = 1024
    whole = lambda array: pl.BlockSpec(array.shape, lambda h: (0, 0))
    return pl.pallas_call(
        functools.partial(question_kernel, groups, key_block),
        grid=(heads,),
        in_specs=[
            pl.BlockSpec(memory_space=pltpu.SMEM),
            pl.BlockSpec((rows, HD), lambda h: (0, h)),
            whole(pk), whole(pv), whole(nk), whole(nv),
        ],
        out_specs=pl.BlockSpec((rows, HD), lambda h: (0, h)),
        out_shape=jax.ShapeDtypeStruct(q.shape, jnp.bfloat16),
        scratch_shapes=[
            pltpu.VMEM((passage, 2 * HD), jnp.bfloat16),
            pltpu.VMEM((new, 2 * HD), jnp.bfloat16),
            pltpu.VMEM((rows, 2 * HD), jnp.float32),
            pltpu.VMEM((rows, HD), jnp.float32),
        ],
        compiler_params=pltpu.CompilerParams(vmem_limit_bytes=48 * 2 ** 20),
        cost_estimate=pl.CostEstimate(
            flops=6 * rows * heads * HD * (passage + new // 2),
            bytes_accessed=8 * rows * columns,
            transcendentals=rows * heads * (passage + new // 2),
        ),
    )(z_index, q, pk, pv, nk, nv)


def passage_kernel(at_once, q_ref, k_ref, v_ref, sq_ref, sk_ref, o_ref, va, bias):
    rows = q_ref.shape[0]
    keys = k_ref.shape[0]
    heads = q_ref.shape[1] // HD

    @pl.when(pl.program_id(0) == 0)
    def _():
        here = lax.broadcasted_iota(jnp.int32, (rows, keys), 0) + (keys - rows)
        there = lax.broadcasted_iota(jnp.int32, (rows, keys), 1)
        seen = (there <= here) & (sq_ref[...] == sk_ref[...])
        bias[...] = jnp.where(seen, 0.0, NEG)
        va[:, HD:] = jnp.ones((keys, HD), jnp.bfloat16)

    va[:, :HD] = v_ref[...]

    def scored(g):
        q = jnp.concatenate([q_ref[:, h * HD:(h + 1) * HD] for h in range(g, g + at_once)], axis=0)
        return scores_of(q, k_ref[...])

    s = scored(0)
    for g in range(0, heads, at_once):
        later = scored(g + at_once) if g + at_once < heads else None
        s = (s.reshape(at_once, rows, keys) + bias[...][None]).reshape(at_once * rows, keys)
        best = jnp.max(s, axis=1, keepdims=True)
        p = jnp.exp2(s * SCALE - best * SCALE).astype(jnp.bfloat16)
        part = jnp.dot(p, va[...], preferred_element_type=jnp.float32)
        out = (part[:, :HD] / part[:, HD:]).astype(jnp.bfloat16)
        for h in range(at_once):
            o_ref[:, (g + h) * HD:(g + h + 1) * HD] = out[h * rows:(h + 1) * rows]
        s = later


def passage_attention(q, keys, values, seg_q, seg_k):
    rows = q.shape[0]
    window = keys.shape[0]
    share = QH // KVH * HD
    return pl.pallas_call(
        functools.partial(passage_kernel, 4),
        grid=(KVH,),
        in_specs=[
            pl.BlockSpec((rows, share), lambda j: (0, j)),
            pl.BlockSpec((window, HD), lambda j: (0, j)),
            pl.BlockSpec((window, HD), lambda j: (0, j)),
            pl.BlockSpec((rows, 1), lambda j: (0, 0)),
            pl.BlockSpec((1, window), lambda j: (0, 0)),
        ],
        out_specs=pl.BlockSpec((rows, share), lambda j: (0, j)),
        out_shape=jax.ShapeDtypeStruct(q.shape, jnp.bfloat16),
        scratch_shapes=[
            pltpu.VMEM((window, 2 * HD), jnp.bfloat16),
            pltpu.VMEM((rows, window), jnp.float32),
        ],
        compiler_params=pltpu.CompilerParams(vmem_limit_bytes=48 * 2 ** 20),
        cost_estimate=pl.CostEstimate(
            flops=6 * rows * QH * HD * window,
            bytes_accessed=4 * rows * QH * HD,
            transcendentals=rows * QH * window,
        ),
    )(q, keys, values, seg_q[:, None], seg_k[None, :])


def on_device(passage_q, passage_k, passage_v, new_q, new_k, new_v, segments):
    lines = lax.axis_size("line")
    plane = lax.axis_size("ctx") * CORES
    ctx_count = lax.axis_size("ctx")
    z_index = lax.axis_index("line")
    everyone = ("ctx", "line", "core")
    total = plane * lines
    flat = (lax.axis_index("ctx") * lines + z_index) * CORES + lax.axis_index("core")
    copies = plane // KVH
    prow, nrow = passage_k.shape[0], new_k.shape[0]

    def swap(array):
        return lax.all_to_all(array, ("ctx", "core"), split_axis=1, concat_axis=0, tiled=True)

    kv = jnp.concatenate(
        [jnp.concatenate([passage_k, new_k], axis=0).reshape(prow + nrow, KVH, HD),
         jnp.concatenate([passage_v, new_v], axis=0).reshape(prow + nrow, KVH, HD)], axis=2)
    kv = jnp.repeat(kv, copies, axis=1).reshape(prow + nrow, plane * 2 * HD)
    kv = swap(kv)
    q = swap(new_q)
    gathered = lax.all_gather(kv, "line", axis=0, tiled=True)
    gathered = gathered.reshape(lines, ctx_count, CORES, prow + nrow, 2 * HD)
    pk = gathered[:, :, :, :prow, :HD].reshape(-1, HD)
    pv = gathered[:, :, :, :prow, HD:].reshape(-1, HD)
    fresh = jnp.transpose(gathered[:, :, :, prow:, :], (1, 0, 2, 3, 4))
    nk = fresh[..., :HD].reshape(-1, HD)
    nv = fresh[..., HD:].reshape(-1, HD)

    hops = -(-(MOST - 1) // prow)
    pair = jnp.concatenate([passage_k, passage_v], axis=1)
    pieces = [
        lax.ppermute(pair, everyone, [(i - d, i) for i in range(d, total)]) for d in range(hops, 0, -1)
    ]
    around = jnp.concatenate(pieces + [pair], axis=0)
    window = hops * prow
    padded = jnp.concatenate([jnp.full((window,), -1, jnp.int32), segments])
    seg_k = lax.dynamic_slice_in_dim(padded, flat * prow, window + prow, 0)
    out_new = question_attention(z_index[None].astype(jnp.int32), q, pk, pv, nk, nv, ctx_count)
    out_new = lax.all_to_all(out_new, ("ctx", "core"), split_axis=0, concat_axis=1, tiled=True)
    out_pass = passage_attention(
        passage_q, around[:, :KVH * HD], around[:, KVH * HD:], seg_k[window:], seg_k)
    return out_pass, out_new


def solution(mesh):
    ctx, head = mesh.devices.shape
    finer = Mesh(mesh.devices.reshape(ctx, head // CORES, CORES), ("ctx", "line", "core"))
    split = P(("ctx", "line", "core"), None)
    return jax.shard_map(
        on_device, mesh=finer, in_specs=(split,) * 6 + (P(),), out_specs=(split, split), check_vma=False
    )
```

time: 822 us -> 263 us (0.32)
  matrix products: 230 us -> 0 us
  other arithmetic: 136 us -> 2.19 us
  waiting for transfers between devices: 211 us -> 96 us
  Pallas kernels: 0 us -> 90.9 us
  local copies, waits for them, and re-layouts: 94.5 us -> 18.6 us
  blocking collectives: 64.5 us -> 17.8 us
  starting transfers between devices: 61.6 us -> 22.4 us
    dot_general x24 -> x0, matrix products: 190 us -> none  [the longest x16 122 us: attend(): jnp.einsum('qhk,kd->qhd', weights.astype(jnp.bfloat16), v_block, preferre...]
    all_to_all x7 -> x2, waiting for transfers between devices: 158 us -> 0.01 us  [the longest x1 0.01 us: swap(): lax.all_to_all(array, ('ctx', 'core'), split_axis=1, concat_axis=0, tiled...]
    reduce_sum x10 -> x0, other arithmetic: 105 us -> none  [the longest x8 73 us: attend(): row_sum = jnp.sum(weights, axis=-1)]
    pallas_call x0 -> x2, Pallas kernels: none -> 90.9 us  [the longest x1 68.4 us: question_attention(): pl.pallas_call(functools.partial(question_kernel, groups, key_block), gri...]
    all_to_all x2 -> x1, blocking collectives: 64.5 us -> 17.8 us  [swap(): lax.all_to_all(array, ('ctx', 'core'), split_axis=1, concat_axis=0, tiled...]
    sub x8 -> x0, matrix products: 39.7 us -> none  [attend(): masked - row_max[..., None]]
    all_gather x1, waiting for transfers between devices: 49.3 us -> 82.1 us  [on_device(): gathered = lax.all_gather(kv, 'line', axis=0, tiled=True)]
    unnamed x34 -> x20, local copies, waits for them, and re-layouts: 31.2 us -> 9.63 us
  transfers between devices with their start and end apart: 16 -> 7, of which waited for: 9 -> 2; matrix products, arithmetic and copies ran while one was open for 16% -> 6% of each run, Pallas kernels for 0% -> 35%
where the time goes in v1:
time: 263 us; the launch traced here: 262 us
  waiting for transfers between devices  96 us (37%)
  Pallas kernels  90.9 us (35%)
  starting transfers between devices  22.4 us (9%)
  local copies, waits for them, and re-layouts  18.6 us (7%)
  blocking collectives  17.8 us (7%)
  between operations  14.2 us (5%)
    all_gather x1, waiting for transfers between devices, on_device(): gathered = lax.all_gather(kv, 'line', axis=0, tiled=True)  82.1 us
    pallas_call x1, Pallas kernels, question_attention(): pl.pallas_call(functools.partial(question_kernel, groups, key_block), gri...  68.4 us
    pallas_call x1, Pallas kernels, passage_attention(): pl.pallas_call(functools.partial(passage_kernel, 4), grid=(KVH,), in_spec...  22.5 us
    all_to_all x1, blocking collectives, swap(): lax.all_to_all(array, ('ctx', 'core'), split_axis=1, concat_axis=0, tiled...  17.8 us
    ppermute x4, starting transfers between devices, on_device(): lax.ppermute(pair, everyone, [(i - d, i) for i in range(d, total)])  14.3 us
    ppermute x4, waiting for transfers between devices, on_device(): lax.ppermute(pair, everyone, [(i - d, i) for i in range(d, total)])  13.9 us
    unnamed x20, local copies, waits for them, and re-layouts  9.63 us
  transfers between devices with their start and end apart: 7, of which 2 were waited for; matrix products, arithmetic and copies ran while one was open for 6% of the time, Pallas kernels for 35%

profile of v1, /device:TPU:0, one launch (start us, length us, event | category | flops | bytes accessed | tf_op | source)
XLA Modules:
  0.0 262.0 jit_solution(6554380397205634441)
XLA Ops:
  7.2 1.0 maximum_bitcast_fusion
  8.3 1.1 maximum_bitcast_fusion.1
  9.5 0.1 pad_maximum_fusion
  9.6 0.2 copy.27
  9.7 17.8 %all_to_all.54 = bf16[192,8,256]{2,0,1:T(8,128)(2,1)} all-to-all(bf16[192,8,256]{2,0,1:T(8,128)(2,1)S(1)} %copy.27), channel_id=1, replica_groups=mesh['ctx'=4,'line'=4,'core'=2] {'ctx','core'}, dimensions={1} | all-to-all | bytes 1572864 | tf_op jit(solution)/shard_map/all_to_all | solution.py:177
  27.5 1.5 copy.36
  29.0 4.5 %all-to-all-start = ((bf16[64,8,2048]{2,0,1:T(8,128)(2,1)}), bf16[64,8,2048]{2,0,1:T(8,128)(2,1)}, u32[]{:S(2)}, u32[]{:S(2)}) async-start(bf16[64,8,2048]{2,0,1:T(8,128)(2,1)} %bitcast.29), calls=%async_computation | async-start | bytes 4194304 | tf_op jit(solution)/shard_map/all_to_all | solution.py:177
  33.5 0.8 constant_dynamic-update-slice_fusion.1
  34.3 0.7 constant_dynamic-update-slice_fusion
  35.0 4.5 %collective-permute-start = (bf16[128,2048]{1,0:T(8,128)(2,1)}, bf16[128,2048]{1,0:T(8,128)(2,1)S(1)}, u32[]{:S(2)}, u32[]{:S(2)}) collective-permute-start(bf16[128,2048]{1,0:T(8,128)(2,1)} %constant_dynamic-update-slice_fusion), channel_id=1, source_target_pairs={{0,4},{1,5},{2,6},{3,7},{4,8},{5,9},{6,10},{7,11},{8,12},{9,13},{1... | collective-permute-start | bytes 1572872 | tf_op jit(solution)/shard_map/ppermute | solution.py:196
  39.5 2.8 %collective-permute-start.3 = (bf16[128,2048]{1,0:T(8,128)(2,1)}, bf16[128,2048]{1,0:T(8,128)(2,1)}, u32[]{:S(2)}, u32[]{:S(2)}) collective-permute-start(bf16[128,2048]{1,0:T(8,128)(2,1)} %constant_dynamic-update-slice_fusion), channel_id=1, source_target_pairs={{0,1},{1,2},{2,3},{3,4},{4,5},{5,6},{6,7},{7,8},{8,9},{9,10},{10,1... | collective-permute-start | bytes 1572872 | tf_op jit(solution)/shard_map/ppermute | solution.py:196
  42.3 3.5 %collective-permute-start.2 = (bf16[128,2048]{1,0:T(8,128)(2,1)}, bf16[128,2048]{1,0:T(8,128)(2,1)}, u32[]{:S(2)}, u32[]{:S(2)}) collective-permute-start(bf16[128,2048]{1,0:T(8,128)(2,1)} %constant_dynamic-update-slice_fusion), channel_id=1, source_target_pairs={{0,2},{1,3},{2,4},{3,5},{4,6},{5,7},{6,8},{7,9},{8,10},{9,11},{10,... | collective-permute-start | bytes 1572872 | tf_op jit(solution)/shard_map/ppermute | solution.py:196
  45.8 3.4 %collective-permute-start.1 = (bf16[128,2048]{1,0:T(8,128)(2,1)}, bf16[128,2048]{1,0:T(8,128)(2,1)}, u32[]{:S(2)}, u32[]{:S(2)}) collective-permute-start(bf16[128,2048]{1,0:T(8,128)(2,1)} %constant_dynamic-update-slice_fusion), channel_id=1, source_target_pairs={{0,3},{1,4},{2,5},{3,6},{4,7},{5,8},{6,9},{7,10},{8,11},{9,12},{10... | collective-permute-start | bytes 1572872 | tf_op jit(solution)/shard_map/ppermute | solution.py:196
  49.3 0.1 pad_dynamic-slice_fusion
  49.3 0.1 copy.25.sq_ref
  49.5 13.9 %collective-permute-done = bf16[128,2048]{1,0:T(8,128)(2,1)S(1)} collective-permute-done((bf16[128,2048]{1,0:T(8,128)(2,1)}, bf16[128,2048]{1,0:T(8,128)(2,1)S(1)}, u32[]{:S(2)}, u32[]{:S(2)}) %collective-permute-start) | collective-permute-done | bytes 524320 | tf_op jit(solution)/shard_map/ppermute | solution.py:196
  63.3 0.8 constant_dynamic-update-slice_fusion.6
  64.2 82.1 %all-gather.2.cloned.1.call-done = bf16[6144,256]{1,0:T(8,128)(2,1)} async-done(((bf16[1536,256]{1,0:T(8,128)(2,1)}), bf16[6144,256]{1,0:T(8,128)(2,1)}) %all-gather.2.cloned.1.call-update) | async-done | bytes 3145744 | tf_op jit(solution)/shard_map/all_gather | solution.py:185
  146.3 1.3 slice_bitcast_fusion
  147.6 0.3 fusion.2
  148.0 1.5 copy-done
  149.5 0.6 fusion
  150.1 68.4 %shard_map.87 = bf16[512,2048]{1,0:T(8,128)(2,1)} custom-call(s32[1]{0:T(128)} %bitcast.1.z_ref, bf16[512,2048]{1,0:T(8,128)(2,1)} %bitcast.3.q_ref, bf16[4096,128]{1,0:T(8,128)(2,1)S(1)} %bitcast.31, bf16[4096,128]{1,0:T(8,128)(2,1)S(1)} %bitcast.30, bf16[2048,128]{1,0:T(8,128)(2,1)S(1)} %bitcast.33, bf16[2048,128]{1,0:T(8,128)(2,1)S(1)} %bitcast.32), custom_call_target="tpu_custom_call" | custom-call | flops 32212254720 | bytes 8388608 | tf_op jit(solution)/shard_map/pallas_call | solution.py:79
  218.5 3.6 %all-to-all-start.2 = ((bf16[8,64,2048]{2,1,0:T(8,128)(2,1)}), bf16[8,64,2048]{2,1,0:T(8,128)(2,1)S(1)}, u32[]{:S(2)}, u32[]{:S(2)}) async-start(bf16[8,64,2048]{2,1,0:T(8,128)(2,1)} %bitcast.12), calls=%async_computation.2 | async-start | bytes 4194304 | tf_op jit(solution)/shard_map/all_to_all | solution.py:203
  222.1 1.9 constant_dynamic-update-slice_fusion.5
  224.0 1.9 constant_dynamic-update-slice_fusion.4
  225.9 1.9 constant_dynamic-update-slice_fusion.3
  227.8 0.7 constant_dynamic-update-slice_fusion.2
  228.5 0.7 constant_dynamic-update-slice_fusion.7
  229.2 1.9 fusion.1
  231.2 22.5 %shard_map.86 = bf16[128,16384]{1,0:T(8,128)(2,1)} custom-call(bf16[128,16384]{1,0:T(8,128)(2,1)} %q_ref.1, bf16[640,1024]{1,0:T(8,128)(2,1)S(1)} %get-tuple-element.5.k_ref, bf16[640,1024]{1,0:T(8,128)(2,1)S(1)} %get-tuple-element.4.v_ref, s32[128,1]{1,0:T(8,128)S(1)} %copy.25.sq_ref, s32[1,640]{1,0:T(1,128)S(1)} %broadcast_in_dim.11.sk_ref), custom_call_target="tpu_custom_call" | custom-call | flops 8053063680 | bytes 8388608 | tf_op jit(solution)/shard_map/pallas_call | solution.py:140
  253.7 1.5 copy.32
  (24 shorter events, 0.3 us)
Async XLA Ops:
  7.2 139.1 %all-gather.2.cloned.1.call-start = ((), (), s32[]{:S(2)}) async-start(), calls=%async_computation.3 | async-start | bytes 3932160 | tf_op jit(solution)/shard_map/all_gather | solution.py:185
  9.5 18.1 %copy-start.4 = (bf16[64,16384]{1,0:T(8,128)(2,1)S(1)}, bf16[64,16384]{1,0:T(8,128)(2,1)}, u32[]{:S(2)}) copy-start(bf16[64,16384]{1,0:T(8,128)(2,1)} %param.10) | copy-start | bytes 6291460
  29.0 4.5 %copy-start.1 = (bf16[128,1024]{1,0:T(8,128)(2,1)S(1)}, bf16[128,1024]{1,0:T(8,128)(2,1)}, u32[]{:S(2)}) copy-start(bf16[128,1024]{1,0:T(8,128)(2,1)} %param.8) | copy-start | bytes 786436
  29.0 5.3 %copy-start.2 = (bf16[128,1024]{1,0:T(8,128)(2,1)S(1)}, bf16[128,1024]{1,0:T(8,128)(2,1)}, u32[]{:S(2)}) copy-start(bf16[128,1024]{1,0:T(8,128)(2,1)} %param.9) | copy-start | bytes 786436
  29.0 20.3 %copy-start.5 = (s32[4096]{0:T(1024)S(1)}, s32[4096]{0:T(1024)}, u32[]{:S(2)}) copy-start(s32[4096]{0:T(1024)} %param.13) | copy-start | bytes 49156
  29.0 121.1 %all-to-all-start = ((bf16[64,8,2048]{2,0,1:T(8,128)(2,1)}), bf16[64,8,2048]{2,0,1:T(8,128)(2,1)}, u32[]{:S(2)}, u32[]{:S(2)}) async-start(bf16[64,8,2048]{2,0,1:T(8,128)(2,1)} %bitcast.29), calls=%async_computation | async-start | bytes 4194304 | tf_op jit(solution)/shard_map/all_to_all | solution.py:177
  35.0 28.3 %collective-permute-start = (bf16[128,2048]{1,0:T(8,128)(2,1)}, bf16[128,2048]{1,0:T(8,128)(2,1)S(1)}, u32[]{:S(2)}, u32[]{:S(2)}) collective-permute-start(bf16[128,2048]{1,0:T(8,128)(2,1)} %constant_dynamic-update-slice_fusion), channel_id=1, source_target_pairs={{0,4},{1,5},{2,6},{3,7},{4,8},{5,9},{6,10},{7,11},{8,12},{9,13},{1... | collective-permute-start | bytes 1572872 | tf_op jit(solution)/shard_map/ppermute | solution.py:196
  39.5 186.4 %collective-permute-start.3 = (bf16[128,2048]{1,0:T(8,128)(2,1)}, bf16[128,2048]{1,0:T(8,128)(2,1)}, u32[]{:S(2)}, u32[]{:S(2)}) collective-permute-start(bf16[128,2048]{1,0:T(8,128)(2,1)} %constant_dynamic-update-slice_fusion), channel_id=1, source_target_pairs={{0,1},{1,2},{2,3},{3,4},{4,5},{5,6},{6,7},{7,8},{8,9},{9,10},{10,1... | collective-permute-start | bytes 1572872 | tf_op jit(solution)/shard_map/ppermute | solution.py:196
  42.3 181.7 %collective-permute-start.2 = (bf16[128,2048]{1,0:T(8,128)(2,1)}, bf16[128,2048]{1,0:T(8,128)(2,1)}, u32[]{:S(2)}, u32[]{:S(2)}) collective-permute-start(bf16[128,2048]{1,0:T(8,128)(2,1)} %constant_dynamic-update-slice_fusion), channel_id=1, source_target_pairs={{0,2},{1,3},{2,4},{3,5},{4,6},{5,7},{6,8},{7,9},{8,10},{9,11},{10,... | collective-permute-start | bytes 1572872 | tf_op jit(solution)/shard_map/ppermute | solution.py:196
  45.8 176.3 %collective-permute-start.1 = (bf16[128,2048]{1,0:T(8,128)(2,1)}, bf16[128,2048]{1,0:T(8,128)(2,1)}, u32[]{:S(2)}, u32[]{:S(2)}) collective-permute-start(bf16[128,2048]{1,0:T(8,128)(2,1)} %constant_dynamic-update-slice_fusion), channel_id=1, source_target_pairs={{0,3},{1,4},{2,5},{3,6},{4,7},{5,8},{6,9},{7,10},{8,11},{9,12},{10... | collective-permute-start | bytes 1572872 | tf_op jit(solution)/shard_map/ppermute | solution.py:196
  147.6 1.9 copy-start
  218.5 35.3 %all-to-all-start.2 = ((bf16[8,64,2048]{2,1,0:T(8,128)(2,1)}), bf16[8,64,2048]{2,1,0:T(8,128)(2,1)S(1)}, u32[]{:S(2)}, u32[]{:S(2)}) async-start(bf16[8,64,2048]{2,1,0:T(8,128)(2,1)} %bitcast.12), calls=%async_computation.2 | async-start | bytes 4194304 | tf_op jit(solution)/shard_map/all_to_all | solution.py:203
  222.1 6.4 %copy-start.3 = (bf16[128,1024]{1,0:T(8,128)(2,1)S(1)}, bf16[128,1024]{1,0:T(8,128)(2,1)}, u32[]{:S(2)}) copy-start(bf16[128,1024]{1,0:T(8,128)(2,1)} %param.9) | copy-start | bytes 786436
Sparse Core Ops, SparseCore 0:
  27.6 118.6 all-gather.1

commit v2 on v1

v2 whole, which is shorter than its diff:
```python
import functools
import math

import jax
import jax.numpy as jnp
from jax import lax
from jax.experimental import pallas as pl
from jax.experimental.pallas import tpu as pltpu
from jax.sharding import Mesh, PartitionSpec as P

QH = 128
KVH = 8
HD = 128
MOST = 512
CORES = 2
NEG = -1e30
SCALE = HD ** -0.5 * math.log2(math.e)
DIMS_T = (((1,), (1,)), ((), ()))


def scores_of(q, k):
    return lax.dot_general(q, k, DIMS_T, preferred_element_type=jnp.float32)


def question_kernel(
    sizes, nq, pk, pv, nk, nv, out, around, kv, q, acc, top, bias, stage,
    kv_send, kv_recv, q_send, q_recv, line_send, line_recv, halo_send, halo_recv,
    relay_send, relay_recv, out_send, out_recv,
):
    ctx_count, lines, hops = sizes
    plane = ctx_count * CORES
    copies = plane // KVH
    prow, nrow = pk.shape[0], nk.shape[0]
    passage = plane * prow
    rows, width = q.shape
    heads = width // HD
    half = rows // 2
    run = CORES * nrow
    batch = 4
    total = plane * lines
    c, z, k = lax.axis_index("ctx"), lax.axis_index("line"), lax.axis_index("core")
    me = c * CORES + k
    flat = (c * lines + z) * CORES + k

    def peer(p):
        return (p // CORES, z, p % CORES)

    def flat_peer(f):
        return (f // (CORES * lines), f // CORES % lines, f % CORES)

    def remote(src, dst, send, recv, device):
        return pltpu.make_async_remote_copy(
            src_ref=src, dst_ref=dst, send_sem=send, recv_sem=recv,
            device_id=device, device_id_type=pl.DeviceIdType.MESH)

    def at(index, size):
        return pl.ds(pl.multiple_of(index * size, size), size)

    def kv_parts(p):
        column = at(p // copies, HD)
        old = at(me, prow)
        new = pl.ds(pl.multiple_of(passage + me * nrow, nrow), nrow)
        return [
            (pk.at[:, column], kv.at[z, old, 0:HD]),
            (pv.at[:, column], kv.at[z, old, HD:2 * HD]),
            (nk.at[:, column], kv.at[z, new, 0:HD]),
            (nv.at[:, column], kv.at[z, new, HD:2 * HD]),
        ]

    def kv_copies(step):
        p = (me + step) % plane
        return [remote(s, t, kv_send.at[step, n], kv_recv.at[step, n], peer(p))
                for n, (s, t) in enumerate(kv_parts(p))]

    def q_copy(step):
        p = (me + step) % plane
        return remote(nq.at[:, at(p, width)], q.at[at(me, nrow), :], q_send.at[step], q_recv.at[step], peer(p))

    own = [pltpu.make_async_copy(s, t, kv_recv.at[0, n]) for n, (s, t) in enumerate(kv_parts(me))]
    own += [pltpu.make_async_copy(nq.at[:, at(me, width)], q.at[at(me, nrow), :], q_recv.at[0])]
    wide = KVH * HD
    kept = [
        pltpu.make_async_copy(pk, around.at[hops * prow:(hops + 1) * prow, 0:wide], halo_recv.at[0, 0]),
        pltpu.make_async_copy(pv, around.at[hops * prow:(hops + 1) * prow, wide:2 * wide], halo_recv.at[0, 1]),
    ]

    def halo_copies(far):
        first = (hops - far) * prow
        device = flat_peer((flat + far) % total)
        return [
            remote(pk, around.at[first:first + prow, 0:wide], halo_send.at[far, 0], halo_recv.at[far, 0], device),
            remote(pv, around.at[first:first + prow, wide:2 * wide], halo_send.at[far, 1], halo_recv.at[far, 1], device),
        ]

    def relay(n):
        first = (hops - 2 * n - 1) * prow
        return remote(
            around.at[at(hops - 2 * n - 2 * k, prow), :], around.at[first:first + prow, :],
            relay_send.at[n], relay_recv.at[n], (c, z, 1 - k))

    def hop(side, step):
        ahead = 1 - 2 * side
        block = jnp.clip(z - ahead * (step - 1), 0, lines - 1)
        part = kv.at[block, :, 0:2 * HD]
        device = (c, (z + ahead + lines) % lines, k)
        return remote(part, part, line_send.at[side, step], line_recv.at[side, step], device)

    def sends(side, step):
        if side == 0:
            return (z - (step - 1) >= 0) & (z + 1 < lines)
        return (z + (step - 1) < lines) & (z >= 1)

    def receives(side, step):
        return z - step >= 0 if side == 0 else z + step < lines

    def out_copy(group, step):
        p = (me + step) % plane
        size = batch * HD
        return (stage.at[at(p, nrow), at(group, size)], out.at[:, at(me * (heads // batch) + group, size)], p)

    def out_remote(group, step):
        s, t, p = out_copy(group, step)
        return remote(s, t, out_send.at[group, step], out_recv.at[group, step], peer(p))

    def out_local(group):
        s, t, _ = out_copy(group, 0)
        return pltpu.make_async_copy(s, t, out_recv.at[group, 0])

    evens = range(2, hops + 1, 2)
    barrier = pltpu.get_barrier_semaphore()
    greeted = [peer((me + step) % plane) for step in range(1, plane)]
    greeted += [(c, (z + 1) % lines, k), (c, (z + lines - 1) % lines, k)]
    for far in evens:
        greeted += [flat_peer((flat + far) % total), flat_peer((flat + total - far) % total)]
    for device in greeted:
        pl.semaphore_signal(barrier, inc=1, device_id=device, device_id_type=pl.DeviceIdType.MESH)
    pl.semaphore_wait(barrier, len(greeted))

    for step in range(1, plane):
        for copy in kv_copies(step):
            copy.start()
    for copy in own:
        copy.start()
    for step in range(1, plane):
        q_copy(step).start()
    for copy in halo_copies(2) + kept:
        copy.start()

    def clear(h, _):
        acc[h] = jnp.zeros((rows, 2 * HD), jnp.float32)
        top[h] = jnp.full((rows, HD), NEG, jnp.float32)
        return 0

    lax.fori_loop(0, heads, clear, 0)
    for line in range(lines):
        kv[line, :, 2 * HD:] = jnp.ones((kv.shape[1], HD), jnp.bfloat16)

    def exchange(phase):
        for side in range(2):
            @pl.when((phase >= 1) & receives(side, phase))
            def _():
                hop(side, phase).wait_recv()
        for side in range(2):
            @pl.when((phase + 1 < lines) & sends(side, phase + 1))
            def _():
                hop(side, phase + 1).start()

    def turn(phase):
        near = jnp.minimum(z, lines - 1 - z)
        both = phase <= 2 * near
        distance = jnp.where(both, (phase + 1) // 2, phase - near)
        left = jnp.where(both, phase % 2 == 1, z > near)
        return jnp.where(phase == 0, z, jnp.where(left, z - distance, z + distance))

    def masks(block):
        row = lax.broadcasted_iota(jnp.int32, (rows, rows), 0)
        col = lax.broadcasted_iota(jnp.int32, (rows, rows), 1)
        step = (lines - 1) * run
        here = row + row // run * step + z * run
        there = col + col // run * step + block * run
        bias[...] = jnp.where(there <= here, 0.0, NEG)

    def head_block(h, block, last):
        lane = at(h, HD)
        scored = []
        for part in range(2):
            first, new = part * half, (part + 1) * half
            qs = q[first:first + half, lane]
            old_s = scores_of(qs, kv[block, 0:passage, 0:HD])
            new_s = scores_of(qs, kv[block, passage:passage + new, 0:HD]) + bias[first:first + half, 0:new]
            scored.append((first, new, old_s, new_s))
        for first, new, old_s, new_s in scored:
            before = top[h, first:first + half, :]
            best = jnp.maximum(jnp.max(old_s, axis=1, keepdims=True), jnp.max(new_s, axis=1, keepdims=True))
            best = jnp.maximum(before[:, :1], best)
            spread = jnp.broadcast_to(best, (half, HD))
            old_p = jnp.exp2(old_s * SCALE - best * SCALE).astype(jnp.bfloat16)
            new_p = jnp.exp2(new_s * SCALE - best * SCALE).astype(jnp.bfloat16)
            got = jnp.dot(old_p, kv[block, 0:passage, HD:3 * HD], preferred_element_type=jnp.float32)
            got += jnp.dot(new_p, kv[block, passage:passage + new, HD:3 * HD], preferred_element_type=jnp.float32)
            shrink = jnp.exp2((before - spread) * SCALE)
            num = acc[h, first:first + half, 0:HD] * shrink + got[:, :HD]
            den = acc[h, first:first + half, HD:2 * HD] * shrink + got[:, HD:]
            if last:
                stage[first:first + half, lane] = (num / den).astype(jnp.bfloat16)
            else:
                acc[h, first:first + half, 0:HD] = num
                acc[h, first:first + half, HD:2 * HD] = den
                top[h, first:first + half, :] = spread

    for copy in own[:4]:
        copy.wait()
    for step in range(1, plane):
        for copy in kv_copies(step):
            copy.wait_recv()

    def phase_step(phase, _):
        exchange(phase)

        @pl.when(phase == 0)
        def _():
            own[4].wait()
            for step in range(1, plane):
                q_copy(step).wait_recv()

        @pl.when(phase == lines - 2)
        def _():
            for far in evens[1:]:
                for copy in halo_copies(far):
                    copy.start()

        block = turn(phase)
        masks(block)

        def each(h, _):
            head_block(h, block, False)
            return 0

        lax.fori_loop(0, heads, each, 0)
        return 0

    lax.fori_loop(0, lines - 1, phase_step, 0)
    exchange(lines - 1)
    block = turn(lines - 1)
    masks(block)
    groups = heads // batch

    def finish(group, _):
        @pl.when(group == groups - 1)
        def _():
            for copy in kept:
                copy.wait()
            for far in evens:
                for copy in halo_copies(far):
                    copy.wait_recv()
            for n in range(hops // 2):
                relay(n).start()

        def each(i, _):
            head_block(group * batch + i, block, True)
            return 0

        lax.fori_loop(0, batch, each, 0)
        for step in range(1, plane):
            out_remote(group, step).start()
        out_local(group).start()
        return 0

    lax.fori_loop(0, groups, finish, 0)

    for step in range(1, plane):
        for copy in kv_copies(step):
            copy.wait_send()
        q_copy(step).wait_send()
    for step in range(1, lines):
        for side in range(2):
            @pl.when(sends(side, step))
            def _():
                hop(side, step).wait_send()
    for far in evens:
        for copy in halo_copies(far):
            copy.wait_send()
    for n in range(hops // 2):
        relay(n).wait()

    def drain(group, _):
        out_local(group).wait()
        for step in range(1, plane):
            out_remote(group, step).wait()
        return 0

    lax.fori_loop(0, groups, drain, 0)


def question_attention(sizes, nq, pk, pv, nk, nv):
    ctx_count, lines, hops = sizes
    plane = ctx_count * CORES
    prow, nrow = pk.shape[0], nk.shape[0]
    width = nq.shape[1] // plane
    rows, heads = plane * nrow, width // HD
    keys = lines * plane * (prow + nrow)
    groups = heads // 4
    dma = pltpu.SemaphoreType.DMA
    anywhere = pl.BlockSpec(memory_space=pl.ANY)
    return pl.pallas_call(
        functools.partial(question_kernel, sizes),
        in_specs=[anywhere] * 5,
        out_specs=[anywhere] * 2,
        out_shape=[
            jax.ShapeDtypeStruct(nq.shape, jnp.bfloat16),
            jax.ShapeDtypeStruct(((hops + 1) * prow, 2 * KVH * HD), jnp.bfloat16),
        ],
        scratch_shapes=[
            pltpu.VMEM((lines, plane * (prow + nrow), 3 * HD), jnp.bfloat16),
            pltpu.VMEM((rows, width), jnp.bfloat16),
            pltpu.VMEM((heads, rows, 2 * HD), jnp.float32),
            pltpu.VMEM((heads, rows, HD), jnp.float32),
            pltpu.VMEM((rows, rows), jnp.float32),
            pltpu.VMEM((rows, width), jnp.bfloat16),
            dma((plane, 4)), dma((plane, 4)), dma((plane,)), dma((plane,)),
            dma((2, lines)), dma((2, lines)), dma((hops + 1, 2)), dma((hops + 1, 2)),
            dma((hops // 2,)), dma((hops // 2,)), dma((groups, plane)), dma((groups, plane)),
        ],
        compiler_params=pltpu.CompilerParams(
            vmem_limit_bytes=56 * 2 ** 20, collective_id=0, has_side_effects=True),
        cost_estimate=pl.CostEstimate(
            flops=6 * rows * heads * HD * keys, bytes_accessed=8 * rows * width,
            transcendentals=rows * heads * keys),
    )(nq, pk, pv, nk, nv)


def passage_kernel(at_once, q_ref, k_ref, v_ref, sq_ref, sk_ref, o_ref, va, bias):
    rows = q_ref.shape[0]
    keys = k_ref.shape[0]
    heads = q_ref.shape[1] // HD

    @pl.when(pl.program_id(0) == 0)
    def _():
        here = lax.broadcasted_iota(jnp.int32, (rows, keys), 0) + (keys - rows)
        there = lax.broadcasted_iota(jnp.int32, (rows, keys), 1)
        seen = (there <= here) & (sq_ref[...] == sk_ref[...])
        bias[...] = jnp.where(seen, 0.0, NEG)
        va[:, HD:] = jnp.ones((keys, HD), jnp.bfloat16)

    va[:, :HD] = v_ref[...]

    def scored(g):
        q = jnp.concatenate([q_ref[:, h * HD:(h + 1) * HD] for h in range(g, g + at_once)], axis=0)
        return scores_of(q, k_ref[...])

    s = scored(0)
    for g in range(0, heads, at_once):
        later = scored(g + at_once) if g + at_once < heads else None
        s = (s.reshape(at_once, rows, keys) + bias[...][None]).reshape(at_once * rows, keys)
        best = jnp.max(s, axis=1, keepdims=True)
        p = jnp.exp2(s * SCALE - best * SCALE).astype(jnp.bfloat16)
        part = jnp.dot(p, va[...], preferred_element_type=jnp.float32)
        out = (part[:, :HD] / part[:, HD:]).astype(jnp.bfloat16)
        for h in range(at_once):
            o_ref[:, (g + h) * HD:(g + h + 1) * HD] = out[h * rows:(h + 1) * rows]
        s = later


def passage_attention(q, around, seg_q, seg_k):
    rows = q.shape[0]
    window = around.shape[0]
    share = QH // KVH * HD
    return pl.pallas_call(
        functools.partial(passage_kernel, 4),
        grid=(KVH,),
        in_specs=[
            pl.BlockSpec((rows, share), lambda j: (0, j)),
            pl.BlockSpec((window, HD), lambda j: (0, j)),
            pl.BlockSpec((window, HD), lambda j: (0, KVH + j)),
            pl.BlockSpec((rows, 1), lambda j: (0, 0)),
            pl.BlockSpec((1, window), lambda j: (0, 0)),
        ],
        out_specs=pl.BlockSpec((rows, share), lambda j: (0, j)),
        out_shape=jax.ShapeDtypeStruct(q.shape, jnp.bfloat16),
        scratch_shapes=[
            pltpu.VMEM((window, 2 * HD), jnp.bfloat16),
            pltpu.VMEM((rows, window), jnp.float32),
        ],
        compiler_params=pltpu.CompilerParams(vmem_limit_bytes=48 * 2 ** 20),
        cost_estimate=pl.CostEstimate(
            flops=6 * rows * QH * HD * window,
            bytes_accessed=4 * rows * QH * HD,
            transcendentals=rows * QH * window,
        ),
    )(q, around, around, seg_q[:, None], seg_k[None, :])


def on_device(passage_q, passage_k, passage_v, new_q, new_k, new_v, segments):
    lines = lax.axis_size("line")
    ctx_count = lax.axis_size("ctx")
    prow = passage_k.shape[0]
    flat = (lax.axis_index("ctx") * lines + lax.axis_index("line")) * CORES + lax.axis_index("core")
    hops = -(-(MOST - 1) // prow)
    hops += hops % 2
    window = hops * prow
    padded = jnp.concatenate([jnp.full((window,), -1, jnp.int32), segments])
    seg_k = lax.dynamic_slice_in_dim(padded, flat * prow, window + prow, 0)
    out_new, around = question_attention(
        (ctx_count, lines, hops), new_q, passage_k, passage_v, new_k, new_v)
    out_pass = passage_attention(passage_q, around, seg_k[window:], seg_k)
    return out_pass, out_new


def solution(mesh):
    ctx, head = mesh.devices.shape
    finer = Mesh(mesh.devices.reshape(ctx, head // CORES, CORES), ("ctx", "line", "core"))
    split = P(("ctx", "line", "core"), None)
    return jax.shard_map(
        on_device, mesh=finer, in_specs=(split,) * 6 + (P(),), out_specs=(split, split), check_vma=False
    )
```

time: 263 us -> 171 us (0.65)
  waiting for transfers between devices: 96 us -> 0 us
  Pallas kernels: 90.9 us -> 166 us
  starting transfers between devices: 22.4 us -> 0 us
  blocking collectives: 17.8 us -> 0 us
  local copies, waits for them, and re-layouts: 18.6 us -> 3.96 us
  between operations: 14.2 us -> 0.66 us
    all_gather x1 -> x0, waiting for transfers between devices: 82.1 us -> none  [on_device(): gathered = lax.all_gather(kv, 'line', axis=0, tiled=True)]
    pallas_call x1, Pallas kernels: 68.4 us -> 143 us  [question_attention(): pl.pallas_call(functools.partial(question_kernel, sizes), in_specs=[anywh...]
    all_to_all x1 -> x0, blocking collectives: 17.8 us -> none  [swap(): lax.all_to_all(array, ('ctx', 'core'), split_axis=1, concat_axis=0, tiled...]
    ppermute x4 -> x0, starting transfers between devices: 14.3 us -> none  [on_device(): lax.ppermute(pair, everyone, [(i - d, i) for i in range(d, total)])]
    ppermute x4 -> x0, waiting for transfers between devices: 13.9 us -> none  [on_device(): lax.ppermute(pair, everyone, [(i - d, i) for i in range(d, total)])]
    all_to_all x2 -> x0, starting transfers between devices: 8.09 us -> none  [the longest x1 4.48 us: swap(): lax.all_to_all(array, ('ctx', 'core'), split_axis=1, concat_axis=0, tiled...]
    unnamed x20 -> x5, local copies, waits for them, and re-layouts: 9.63 us -> 3.06 us
    slice x5 -> x0, local copies, waits for them, and re-layouts: 2.92 us -> none  [the longest x1 1.95 us: on_device(): around[:, KVH * HD:]]
  transfers between devices with their start and end apart: 7 -> 0, of which waited for: 2 -> 0; matrix products, arithmetic and copies ran while one was open for 6% -> 0% of each run, Pallas kernels for 35% -> 0%
where the time goes in v2:
time: 171 us
  Pallas kernels  166 us (97%)
  local copies, waits for them, and re-layouts  3.96 us (2%)
    pallas_call x1, Pallas kernels, question_attention(): pl.pallas_call(functools.partial(question_kernel, sizes), in_specs=[anywh...  143 us
    pallas_call x1, Pallas kernels, passage_attention(): pl.pallas_call(functools.partial(passage_kernel, 4), grid=(KVH,), in_spec...  22.8 us

profile of v2, /device:TPU:0, one launch (start us, length us, event | category | flops | bytes accessed | tf_op | source)
XLA Modules:
  0.0 170.7 jit_solution(393401015164437236)
XLA Ops:
  0.6 0.8 pad_dynamic-slice_fusion
  1.4 0.1 copy.9.sq_ref
  1.5 143.3 %shard_map.86 = (bf16[64,16384]{1,0:T(8,128)(2,1)}, bf16[640,2048]{1,0:T(8,128)(2,1)}) custom-call(bf16[64,16384]{1,0:T(8,128)(2,1)} %nq.1, bf16[128,1024]{1,0:T(8,128)(2,1)} %pk.1, bf16[128,1024]{1,0:T(8,128)(2,1)} %pv.1, bf16[64,1024]{1,0:T(8,128)(2,1)} %nk.1, bf16[64,1024]{1,0:T(8,128)(2,1)} %nv.1), custom_call_target="tpu_custom_call" | custom-call | flops 38654705664 | bytes 8388608 | tf_op jit(solution)/shard_map/pallas_call | solution.py:305
  144.9 0.0 copy-start
  144.9 1.7 %copy-done = bf16[640,2048]{1,0:T(8,128)(2,1)S(1)} copy-done((bf16[640,2048]{1,0:T(8,128)(2,1)S(1)}, bf16[640,2048]{1,0:T(8,128)(2,1)}, u32[]{:S(2)}) %copy-start) | copy-done | bytes 2621464
  146.6 0.0 copy-start.1
  146.6 22.8 %shard_map.87 = bf16[128,16384]{1,0:T(8,128)(2,1)} custom-call(bf16[128,16384]{1,0:T(8,128)(2,1)} %q_ref.1, bf16[640,2048]{1,0:T(8,128)(2,1)S(1)} %copy-done, bf16[640,2048]{1,0:T(8,128)(2,1)S(1)} %copy-done, s32[128,1]{1,0:T(8,128)S(1)} %copy.9.sq_ref, s32[1,640]{1,0:T(1,128)S(1)} %broadcast_in_dim.8.sk_ref), custom_call_target="tpu_custom_call" | custom-call | flops 8053063680 | bytes 8388608 | tf_op jit(solution)/shard_map/pallas_call | solution.py:368
  169.4 0.0 copy-done.1
  169.4 1.3 copy.11
  (2 shorter events, 0.0 us)
Async XLA Ops:
  144.9 1.7 %copy-start = (bf16[640,2048]{1,0:T(8,128)(2,1)S(1)}, bf16[640,2048]{1,0:T(8,128)(2,1)}, u32[]{:S(2)}) copy-start(bf16[640,2048]{1,0:T(8,128)(2,1)} %get-tuple-element.4.k_ref.v_ref) | copy-start | bytes 7864324
  146.6 22.8 %copy-start.1 = (bf16[64,16384]{1,0:T(8,128)(2,1)S(1)}, bf16[64,16384]{1,0:T(8,128)(2,1)}, u32[]{:S(2)}) copy-start(bf16[64,16384]{1,0:T(8,128)(2,1)} %get-tuple-element.9) | copy-start | bytes 6291460
